TPU v7x, 32 devices: a whole 2x2x4 slice. The times are simulated.
32 devices in a mesh: section: 2 (over core), ctx: 16 (over z, y, x).
Axes of the slice: x: 2, y: 2, z: 4, core: 2. Of those that a mesh axis runs over, the one named last changes fastest.
Arguments:
- hidden_in: bfloat16 [4096, 8192], P('ctx'), may hold values from -3 to 3
- query_rows: bfloat16 [2, 4096, 8192], P('section', 'ctx'), may hold values from -6 to 6
- key_rows: bfloat16 [2, 4096, 1024], P('section', 'ctx'), may hold values from -6 to 6
- value_rows: bfloat16 [2, 4096, 1024], P('section', 'ctx'), may hold values from -24 to 24
- stretch_len: int32 [16], replicated, may hold values from 128 to 256, as said below
- segment_ids: int32 [4096], P('ctx'), may hold values from 0 to 34, as said below
Outputs:
- hidden_out: bfloat16 [2, 4096, 8192], P('section', 'ctx')
Inputs may be any that keep to these rules, and one draw needn't show every extreme that they name: stretch_len values are multiples of 128; stretch_len[0] = 256 and the last entry is 128. `segment_ids`: segment ids never fall along the slots; exactly the first 128 slots carry 0; each candidate solution covers at most 1536 consecutive slots, and one covers exactly that many; the last slot carries the largest id.
All inputs are finite; a program needn't handle non-finite values.
Results may differ from a plain program's by a relative error of at most 0.005.
Values may be sent and summed in bfloat16 or wider, within the bound.
A program may use at most 320 MiB of HBM per device.

v0:
```python
import jax
import jax.numpy as jnp
from jax import lax
from jax.sharding import PartitionSpec as P

D = 8192
QH = 64
KVH = 8
HD = 128
REACH = 6


NEG_FILL = -1e30


def spread(array, axis, root):
    mine = lax.axis_index(axis) == root
    return lax.psum(jnp.where(mine, array, jnp.zeros_like(array)), axis)


def passed_along(array, axis, by):
    size = lax.axis_size(axis)
    pairs = [(i, i + by) for i in range(size) if 0 <= i + by < size]
    return lax.ppermute(array, axis, pairs)


def fold_block(running, query_heads, key_block, value_block, visible):
    top_score, totals, mixed_sum = running
    key_heads = key_block.reshape(key_block.shape[0], KVH, HD)
    value_heads = value_block.reshape(value_block.shape[0], KVH, HD)
    scores = jnp.einsum(
        "tkgd,skd->kgts", query_heads, key_heads, preferred_element_type=jnp.float32
    ) * HD ** (-0.5)
    scores = jnp.where(visible, scores, NEG_FILL)
    new_top = jnp.maximum(top_score, jnp.max(scores, axis=-1))
    weights = jnp.where(visible, jnp.exp(scores - new_top[..., None]), 0.0)
    factor = jnp.exp(top_score - new_top)
    totals = totals * factor + jnp.sum(weights, axis=-1)
    update = jnp.einsum(
        "kgts,skd->tkgd",
        weights.astype(jnp.bfloat16),
        value_heads,
        preferred_element_type=jnp.float32,
    )
    mixed_sum = mixed_sum * jnp.transpose(factor, (2, 0, 1))[..., None] + update
    return (new_top, totals, mixed_sum)


def maybe_fold(running, query_heads, key_packet, visible):
    return fold_block(running, query_heads, key_packet[0], key_packet[1], visible)


def local(hidden_in, query_rows, key_rows, value_rows, stretch_len, segment_ids):
    tok_count = hidden_in.shape[0]
    groups = QH // KVH
    device = lax.axis_index("ctx")
    section_index = lax.axis_index("section")
    slot_rows = jnp.arange(tok_count, dtype=jnp.int32)
    query_valid = slot_rows < stretch_len[device]
    query_heads = query_rows[0].reshape(tok_count, KVH, groups, HD)
    packet = (key_rows[0], value_rows[0], segment_ids)
    running = (
        jnp.full((KVH, groups, tok_count), NEG_FILL, jnp.float32),
        jnp.zeros((KVH, groups, tok_count), jnp.float32),
        jnp.zeros((tok_count, KVH, groups, HD), jnp.float32),
    )
    own_visible = (
        query_valid[None, :]
        & (slot_rows[None, :] <= slot_rows[:, None])
        & (segment_ids[None, :] == segment_ids[:, None])
    )
    running = fold_block(running, query_heads, key_rows[0], value_rows[0], own_visible)
    prompt = (spread(packet[0], "ctx", 0), spread(packet[1], "ctx", 0), spread(packet[2], "ctx", 0))
    prompt_visible = (
        (slot_rows < stretch_len[0])[None, :]
        & (prompt[2] == 0)[None, :]
        & (segment_ids != 0)[:, None]
    )
    running = maybe_fold(running, query_heads, prompt, prompt_visible)
    received = []
    moving = packet
    for offset in range(1, REACH + 1):
        moving = passed_along((moving[0], moving[1], moving[2]), "ctx", 1)
        received.append((offset, moving))
    for offset, key_packet in received:
        source = device - offset
        key_valid = (slot_rows < stretch_len[jnp.maximum(source, 0)]) & (source >= 0)
        visible = key_valid[None, :] & (key_packet[2][None, :] == segment_ids[:, None])
        running = maybe_fold(running, query_heads, key_packet, visible)
    top_score, totals, mixed_sum = running
    context = (mixed_sum / jnp.transpose(totals, (2, 0, 1))[..., None]).reshape(tok_count, D)
    context = jnp.where(query_valid[:, None], context, 0.0)
    base_rows = (hidden_in.astype(jnp.float32) + context).astype(jnp.bfloat16)
    passed = passed_along(base_rows, "section", 1)
    result = jnp.where(
        section_index == 0, base_rows, (passed.astype(jnp.float32) + context).astype(jnp.bfloat16)
    )
    return result[None]


def solution(mesh):
    return jax.shard_map(
        local,
        mesh=mesh,
        in_specs=(
            P("ctx", None),
            P("section", "ctx", None),
            P("section", "ctx", None),
            P("section", "ctx", None),
            P(),
            P("ctx"),
        ),
        out_specs=P("section", "ctx", None),
        check_vma=False,
    )
```

profile of v0, /device:TPU:17, one launch (start us, length us, event | category | flops | bytes accessed | tf_op | source)
XLA Modules:
  0.0 457.1 jit_solution(7304560137324435093)
XLA Ops:
  23.4 21.0 %psum.21 = s32[256]{0:T(256)S(1)} all-reduce(s32[256]{0:T(256)S(1)} %broadcast_select_fusion.2), channel_id=1, replica_groups=mesh['section'=2,'ctx'=16] {'ctx'}, use_global_device_ids=true, to_apply=%region_1.2 | all-reduce | flops 256 | bytes 2048 | tf_op jit(solution)/shard_map/psum | solution.py:18
  83.0 9.8 %fusion = (f32[8,8,256]{2,1,0:T(8,128)}, f32[8,256,256,8]{2,1,3,0:T(8,128)}) fusion(pred[256,256]{0,1:T(8,128)(4,1)S(1)} %get-tuple-element.26, bf16[256,8,8,128]{3,2,1,0:T(8,128)(2,1)S(1)} %bitcast.367, bf16[256,8,128,1]{2,1,0,3:T(8,128)(2,1)S(1)} %bitcast.377), kind=kOutput, calls=%fused_computation.16 | convolution fusion | flops 1086308352 | bytes 21626880 | tf_op jit(solution)/shard_map/tkgd,skd->kgts/dot_general | solution.py:31
  96.9 14.6 %fusion.2 = (f32[8,8,256]{2,1,0:T(8,128)}, f32[8,256,256,8]{2,1,3,0:T(8,128)}) fusion(pred[256,256]{0,1:T(8,128)(4,1)S(1)} %get-tuple-element.32, bf16[256,8,128,1]{0,2,3,1:T(8,128)(2,1)} %bitcast.89, bf16[256,8,8,128]{3,2,1,0:T(8,128)(2,1)S(1)} %bitcast.368), kind=kOutput, calls=%fused_computation.18 | convolution fusion | flops 1086308352 | bytes 21626880 | tf_op jit(solution)/shard_map/tkgd,skd->kgts/dot_general | solution.py:31
  111.5 27.0 %all-reduce.3.cloned.1.call-done = (bf16[256,8,128]{2,0,1:T(8,128)(2,1)}, bf16[256,8,128]{0,2,1:T(8,128)(2,1)}) async-done(((bf16[256,8,128]{2,0,1:T(8,128)(2,1)}, bf16[256,8,128]{0,2,1:T(8,128)(2,1)}), (bf16[256,8,128]{2,0,1:T(8,128)(2,1)}, bf16[256,8,128]{0,2,1:T(8,128)(2,1)})) %all-reduce.3.cloned.1.call-update) | async-done | bytes 1048592 | tf_op jit(solution)/shard_map/psum | solution.py:18
  152.8 14.0 %fusion.3 = (f32[8,8,256]{2,1,0:T(8,128)S(1)}, f32[8,256,256,8]{2,1,3,0:T(8,128)}) fusion(pred[256,256]{0,1:T(8,128)(4,1)S(1)} %copy-done.21, bf16[256,8,128,1]{0,2,3,1:T(8,128)(2,1)} %bitcast.93, bf16[256,8,8,128]{3,2,1,0:T(8,128)(2,1)S(1)} %bitcast.370), kind=kOutput, calls=%fused_computation.19 | convolution fusion | flops 1086308352 | bytes 21626880 | tf_op jit(solution)/shard_map/tkgd,skd->kgts/dot_general | solution.py:31
  174.5 9.2 %fusion.4 = (f32[8,8,256]{2,1,0:T(8,128)S(1)}, f32[8,256,256,8]{2,1,3,0:T(8,128)}) fusion(pred[256,256]{0,1:T(8,128)(4,1)S(1)} %copy-done.19, bf16[256,8,128,1]{0,2,3,1:T(8,128)(2,1)S(1)} %bitcast.384, bf16[256,8,8,128]{3,2,1,0:T(8,128)(2,1)S(1)} %bitcast.371), kind=kOutput, calls=%fused_computation.20 | convolution fusion | flops 1086308352 | bytes 21626880 | tf_op jit(solution)/shard_map/tkgd,skd->kgts/dot_general | solution.py:31
  197.6 9.2 %fusion.5 = (f32[8,8,256]{2,1,0:T(8,128)S(1)}, f32[8,256,256,8]{2,1,3,0:T(8,128)}) fusion(pred[256,256]{0,1:T(8,128)(4,1)S(1)} %copy-done.17, bf16[256,8,128,1]{0,2,3,1:T(8,128)(2,1)S(1)} %bitcast.385, bf16[256,8,8,128]{3,2,1,0:T(8,128)(2,1)S(1)} %bitcast.372), kind=kOutput, calls=%fused_computation.21 | convolution fusion | flops 1086308352 | bytes 21626880 | tf_op jit(solution)/shard_map/tkgd,skd->kgts/dot_general | solution.py:31
  220.7 9.2 %fusion.6 = (f32[8,8,256]{2,1,0:T(8,128)S(1)}, f32[8,256,256,8]{2,1,3,0:T(8,128)}) fusion(pred[256,256]{0,1:T(8,128)(4,1)S(1)} %copy-done.15, bf16[256,8,128,1]{0,2,3,1:T(8,128)(2,1)S(1)} %bitcast.386, bf16[256,8,8,128]{3,2,1,0:T(8,128)(2,1)S(1)} %bitcast.373), kind=kOutput, calls=%fused_computation.22 | convolution fusion | flops 1086308352 | bytes 21626880 | tf_op jit(solution)/shard_map/tkgd,skd->kgts/dot_general | solution.py:31
  229.9 9.2 %fusion.7 = (f32[8,8,256]{2,1,0:T(8,128)S(1)}, f32[8,256,256,8]{2,1,3,0:T(8,128)}) fusion(pred[256,256]{0,1:T(8,128)(4,1)S(1)} %copy-done.13, bf16[256,8,128,1]{0,2,3,1:T(8,128)(2,1)S(1)} %bitcast.387, bf16[256,8,8,128]{3,2,1,0:T(8,128)(2,1)S(1)} %bitcast.374), kind=kOutput, calls=%fused_computation.23 | convolution fusion | flops 1086308352 | bytes 21626880 | tf_op jit(solution)/shard_map/tkgd,skd->kgts/dot_general | solution.py:31
  239.6 13.3 %fusion.34 = f32[8,8,256,128]{2,3,1,0:T(8,128)} fusion(bf16[256,8,128,1]{0,2,3,1:T(8,128)(2,1)} %bitcast.27, f32[8,256,256,8]{2,1,3,0:T(8,128)} %get-tuple-element.52, f32[8,8,256]{2,1,0:T(8,128)S(1)} %get-tuple-element.21, pred[256,256]{0,1:T(8,128)(4,1)} %copy-done.23), kind=kOutput, calls=%fused_computation.45 | convolution fusion | flops 1094713344 | bytes 25821184 | tf_op jit(solution)/shard_map/kgts,skd->tkgd/dot_general | solution.py:39
  253.0 14.3 %fusion.8 = (f32[8,8,256]{2,1,0:T(8,128)S(1)}, f32[8,8,256]{2,1,0:T(8,128)S(1)}) fusion(f32[8,256,256,8]{2,1,3,0:T(8,128)} %get-tuple-element.56, f32[8,8,256]{2,1,0:T(8,128)S(1)} %get-tuple-element.25, pred[256,256]{0,1:T(8,128)(4,1)S(1)} %copy-done.6, f32[8,8,256]{2,1,0:T(8,128)S(1)} %get-tuple-element.21, f32[8,256,256,8]{2,1,3,0:T(8,128)} %get-tuple-element.52, ...), kind=kLoop, calls=%fused_computation.24 | loop fusion | flops 41910272 | bytes 33947648 | tf_op jit(solution)/shard_map/reduce_sum | solution.py:38
  267.3 13.3 %fusion.38 = f32[8,8,256,128]{2,3,1,0:T(8,128)} fusion(bf16[256,8,128,1]{0,2,3,1:T(8,128)(2,1)S(1)} %bitcast.380, f32[8,256,256,8]{2,1,3,0:T(8,128)} %get-tuple-element.56, f32[8,8,256]{2,1,0:T(8,128)S(1)} %get-tuple-element.25, pred[256,256]{0,1:T(8,128)(4,1)S(1)} %copy-done.6), kind=kOutput, calls=%fused_computation.47 | convolution fusion | flops 1094713344 | bytes 25821184 | tf_op jit(solution)/shard_map/kgts,skd->tkgd/dot_general | solution.py:39
  280.7 13.5 %fusion.32 = f32[8,8,256,128]{2,3,1,0:T(8,128)} fusion(bf16[256,8,128,1]{0,2,3,1:T(8,128)(2,1)} %bitcast.36, f32[8,256,256,8]{2,1,3,0:T(8,128)} %get-tuple-element.50, f32[8,8,256]{2,1,0:T(8,128)S(1)} %get-tuple-element.20, pred[256,256]{0,1:T(8,128)(4,1)S(1)} %copy-done.22), kind=kOutput, calls=%fused_computation.44 | convolution fusion | flops 1094713344 | bytes 25821184 | tf_op jit(solution)/shard_map/kgts,skd->tkgd/dot_general | solution.py:39
  294.2 14.3 %fusion.14 = (f32[8,8,256]{2,1,0:T(8,128)S(1)}, f32[8,8,256]{2,1,0:T(8,128)S(1)}) fusion(f32[8,256,256,8]{2,1,3,0:T(8,128)} %get-tuple-element.50, f32[8,8,256]{2,1,0:T(8,128)S(1)} %get-tuple-element.20, pred[256,256]{0,1:T(8,128)(4,1)S(1)} %copy-done.22, f32[8,8,256]{2,1,0:T(8,128)S(1)} %get-tuple-element.19, f32[8,256,256,8]{2,1,3,0:T(8,128)} %get-tuple-element.48, ...), kind=kLoop, calls=%fused_computation.30 | loop fusion | flops 41910272 | bytes 33947648 | tf_op jit(solution)/shard_map/reduce_sum | solution.py:38
  308.6 13.4 %fusion.30 = f32[8,8,256,128]{2,3,1,0:T(8,128)} fusion(bf16[256,8,128,1]{0,2,3,1:T(8,128)(2,1)S(1)} %bitcast.388, f32[8,256,256,8]{2,1,3,0:T(8,128)} %get-tuple-element.48, f32[8,8,256]{2,1,0:T(8,128)S(1)} %get-tuple-element.19, pred[256,256]{0,1:T(8,128)(4,1)S(1)} %copy-done.20), kind=kOutput, calls=%fused_computation.43 | convolution fusion | flops 1094713344 | bytes 25821184 | tf_op jit(solution)/shard_map/kgts,skd->tkgd/dot_general | solution.py:39
  322.0 13.3 %fusion.28 = f32[8,8,256,128]{2,3,1,0:T(8,128)} fusion(bf16[256,8,128,1]{0,2,3,1:T(8,128)(2,1)S(1)} %bitcast.389, f32[8,256,256,8]{2,1,3,0:T(8,128)} %get-tuple-element.46, f32[8,8,256]{2,1,0:T(8,128)S(1)} %get-tuple-element.18, pred[256,256]{0,1:T(8,128)(4,1)S(1)} %copy-done.18), kind=kOutput, calls=%fused_computation.42 | convolution fusion | flops 1094713344 | bytes 25821184 | tf_op jit(solution)/shard_map/kgts,skd->tkgd/dot_general | solution.py:39
  335.3 14.4 %fusion.18 = (f32[8,8,256]{2,1,0:T(8,128)S(1)}, f32[8,8,256]{2,1,0:T(8,128)S(1)}) fusion(f32[8,256,256,8]{2,1,3,0:T(8,128)} %get-tuple-element.46, f32[8,8,256]{2,1,0:T(8,128)S(1)} %get-tuple-element.18, pred[256,256]{0,1:T(8,128)(4,1)S(1)} %copy-done.18, f32[8,8,256]{2,1,0:T(8,128)S(1)} %get-tuple-element.17, f32[8,256,256,8]{2,1,3,0:T(8,128)} %get-tuple-element.44, ...), kind=kLoop, calls=%fused_computation.34 | loop fusion | flops 41910272 | bytes 33947648 | tf_op jit(solution)/shard_map/reduce_sum | solution.py:38
  356.0 11.4 %fusion.10 = (f32[8,8,256]{2,1,0:T(8,128)S(1)}, f32[8,8,256]{2,1,0:T(8,128)S(1)}) fusion(f32[8,256,256,8]{2,1,3,0:T(8,128)S(1)} %get-tuple-element.54, f32[8,8,256]{2,1,0:T(8,128)S(1)} %get-tuple-element.22, pred[256,256]{0,1:T(8,128)(4,1)S(1)} %copy-done.4, f32[8,8,256]{2,1,0:T(8,128)S(1)} %get-tuple-element.16, f32[8,256,256,8]{2,1,3,0:T(8,128)} %get-tuple-element.42, ...), kind=kLoop, calls=%fused_computation.26 | loop fusion | flops 41910272 | bytes 33947648 | tf_op jit(solution)/shard_map/reduce_sum | solution.py:38
  367.5 13.6 %fusion.26 = f32[8,8,256,128]{2,3,1,0:T(8,128)} fusion(bf16[256,8,128,1]{0,2,3,1:T(8,128)(2,1)} %bitcast.63, f32[8,256,256,8]{2,1,3,0:T(8,128)} %get-tuple-element.44, f32[8,8,256]{2,1,0:T(8,128)S(1)} %get-tuple-element.17, pred[256,256]{0,1:T(8,128)(4,1)S(1)} %copy-done.16), kind=kOutput, calls=%fused_computation.41 | convolution fusion | flops 1094713344 | bytes 25821184 | tf_op jit(solution)/shard_map/kgts,skd->tkgd/dot_general | solution.py:39
  381.3 29.8 %fusion.40 = f32[256,8,8,128]{0,3,2,1:T(8,128)} fusion(f32[8,8,256,128]{2,3,1,0:T(8,128)} %fusion.26, f32[8,8,256,128]{2,3,1,0:T(8,128)} %fusion.28, f32[8,8,256,128]{2,3,1,0:T(8,128)} %fusion.30, f32[8,8,256,128]{2,3,1,0:T(8,128)} %fusion.32, f32[8,8,256,128]{2,3,1,0:T(8,128)} %fusion.34, f32[8,128,8,256]{3,1,2,0:T(8,128)} %fusion.36, ...), kind=kOutput, calls=%fused_computation.49 | convolution fusion | flops 1128267776 | bytes 85131264 | tf_op jit(solution)/shard_map/kgts,skd->tkgd/dot_general | solution.py:39
  411.1 8.9 %copy.60 = f32[256,8192]{1,0:T(8,128)} copy(f32[256,8192]{0,1:T(8,128)} %bitcast.375) | data formatting | bytes 16777216 | tf_op jit(solution)/shard_map/reshape | solution.py:91
  420.1 8.1 %add_convert_fusion.1 = bf16[256,8192]{1,0:T(8,128)(2,1)} fusion(bf16[256,8192]{1,0:T(8,128)(2,1)} %param.6, f32[256,8192]{1,0:T(8,128)} %copy.60, pred[256]{0:T(512)(128)(4,1)S(1)} %copy-done.37), kind=kLoop, calls=%fused_computation.65 | loop fusion | flops 8388608 | bytes 16777472 | tf_op jit(solution)/shard_map/convert_element_type | solution.py:93
  429.5 11.4 %collective-permute-done.18 = bf16[256,8192]{1,0:T(8,128)(2,1)} collective-permute-done((bf16[256,8192]{1,0:T(8,128)(2,1)}, bf16[256,8192]{1,0:T(8,128)(2,1)}, u32[]{:S(2)}, u32[]{:S(2)}) %collective-permute-start.18) | collective-permute-done | bytes 4194336 | tf_op jit(solution)/shard_map/ppermute | solution.py:24
  440.9 8.9 %fusion.89 = bf16[1,256,8192]{2,1,0:T(8,128)(2,1)} fusion(f32[256,8192]{1,0:T(8,128)} %copy.60, bf16[256,8192]{1,0:T(8,128)(2,1)} %collective-permute-done.18, pred[256]{0:T(512)(128)(4,1)S(1)} %copy-done.37, pred[]{:T(512)S(6)} %eq.36, bf16[256,8192]{1,0:T(8,128)(2,1)} %param.6), kind=kLoop, calls=%fused_computation.107 | loop fusion | flops 16777216 | bytes 20971776 | tf_op jit(solution)/shard_map/broadcast_in_dim | solution.py:98
  (150 shorter events, 117.2 us)
Async XLA Ops:
  6.5 132.0 %all-reduce.3.cloned.1.call-start = ((), (), s32[]{:S(2)}) async-start(), calls=%async_computation | async-start | bytes 2097152 | tf_op jit(solution)/shard_map/psum | solution.py:18
  6.5 39.8 %collective-permute-start = (s32[256]{0:T(256)}, s32[256]{0:T(256)S(1)}, u32[]{:S(2)}, u32[]{:S(2)}) collective-permute-start(s32[256]{0:T(256)} %param.11), channel_id=1, source_target_pairs={{0,1},{1,2},{2,3},{3,4},{4,5},{5,6},{6,7},{7,8},{8,9},{9,10},{10,1... | collective-permute-start | bytes 3080 | tf_op jit(solution)/shard_map/ppermute | solution.py:24
  10.9 81.9 %collective-permute-start.1 = (bf16[256,1024]{0,1:T(8,128)(2,1)S(1)}, bf16[256,1024]{0,1:T(8,128)(2,1)}, u32[]{:S(2)}, u32[]{:S(2)}) collective-permute-start(bf16[256,1024]{0,1:T(8,128)(2,1)S(1)} %bitcast.382), channel_id=1, source_target_pairs={{0,1},{1,2},{2,3},{3,4},{4,5},{5,6},{6,7},{7,8},{8,9},{9,10},{10,1... | collective-permute-start | bytes 1572872 | tf_op jit(solution)/shard_map/ppermute | solution.py:24
  15.3 77.5 %copy-start.2 = (bf16[1,256,1024]{1,2,0:T(8,128)(2,1)}, bf16[1,256,1024]{1,2,0:T(8,128)(2,1)S(1)}, u32[]{:S(2)}) copy-start(bf16[1,256,1024]{1,2,0:T(8,128)(2,1)S(1)} %copy.87) | copy-start | bytes 1572868
  15.3 79.4 %collective-permute-start.2 = (bf16[256,1024]{0,1:T(8,128)(2,1)S(1)}, bf16[256,1024]{0,1:T(8,128)(2,1)}, u32[]{:S(2)}, u32[]{:S(2)}) collective-permute-start(bf16[256,1024]{0,1:T(8,128)(2,1)S(1)} %bitcast.379), channel_id=1, source_target_pairs={{0,1},{1,2},{2,3},{3,4},{4,5},{5,6},{6,7},{7,8},{8,9},{9,10},{10,1... | collective-permute-start | bytes 1572872 | tf_op jit(solution)/shard_map/ppermute | solution.py:24
  23.4 69.4 %copy-start.36 = (pred[256]{0:T(512)(128)(4,1)}, pred[256]{0:T(512)(128)(4,1)S(1)}, u32[]{:S(2)}) copy-start(pred[256]{0:T(512)(128)(4,1)S(1)} %iota_compare_fusion.1) | copy-start | bytes 772
  46.3 8.7 %collective-permute-start.3 = (s32[256]{0:T(256)S(1)}, s32[256]{0:T(256)S(1)}, u32[]{:S(2)}, u32[]{:S(2)}) collective-permute-start(s32[256]{0:T(256)S(1)} %collective-permute-done), channel_id=1, source_target_pairs={{0,1},{1,2},{2,3},{3,4},{4,5},{5,6},{6,7},{7,8},{8,9},{9,10},{10,1... | collective-permute-start | bytes 3080 | tf_op jit(solution)/shard_map/ppermute | solution.py:24
  55.0 6.1 %collective-permute-start.6 = (s32[256]{0:T(256)S(1)}, s32[256]{0:T(256)S(1)}, u32[]{:S(2)}, u32[]{:S(2)}) collective-permute-start(s32[256]{0:T(256)S(1)} %collective-permute-done.3), channel_id=1, source_target_pairs={{0,1},{1,2},{2,3},{3,4},{4,5},{5,6},{6,7},{7,8},{8,9},{9,10},{10,1... | collective-permute-start | bytes 3080 | tf_op jit(solution)/shard_map/ppermute | solution.py:24
  61.1 6.1 %collective-permute-start.9 = (s32[256]{0:T(256)S(1)}, s32[256]{0:T(256)S(1)}, u32[]{:S(2)}, u32[]{:S(2)}) collective-permute-start(s32[256]{0:T(256)S(1)} %collective-permute-done.6), channel_id=1, source_target_pairs={{0,1},{1,2},{2,3},{3,4},{4,5},{5,6},{6,7},{7,8},{8,9},{9,10},{10,1... | collective-permute-start | bytes 3080 | tf_op jit(solution)/shard_map/ppermute | solution.py:24
  67.2 6.1 %collective-permute-start.12 = (s32[256]{0:T(256)S(1)}, s32[256]{0:T(256)S(1)}, u32[]{:S(2)}, u32[]{:S(2)}) collective-permute-start(s32[256]{0:T(256)S(1)} %collective-permute-done.9), channel_id=1, source_target_pairs={{0,1},{1,2},{2,3},{3,4},{4,5},{5,6},{6,7},{7,8},{8,9},{9,10},{10,1... | collective-permute-start | bytes 3080 | tf_op jit(solution)/shard_map/ppermute | solution.py:24
  73.3 7.5 %collective-permute-start.15 = (s32[256]{0:T(256)S(1)}, s32[256]{0:T(256)S(1)}, u32[]{:S(2)}, u32[]{:S(2)}) collective-permute-start(s32[256]{0:T(256)S(1)} %collective-permute-done.12), channel_id=1, source_target_pairs={{0,1},{1,2},{2,3},{3,4},{4,5},{5,6},{6,7},{7,8},{8,9},{9,10},{10,1... | collective-permute-start | bytes 3080 | tf_op jit(solution)/shard_map/ppermute | solution.py:24
  92.8 53.3 %collective-permute-start.4 = (bf16[256,1024]{0,1:T(8,128)(2,1)}, bf16[256,1024]{0,1:T(8,128)(2,1)}, u32[]{:S(2)}, u32[]{:S(2)}) collective-permute-start(bf16[256,1024]{0,1:T(8,128)(2,1)} %collective-permute-done.1), channel_id=1, source_target_pairs={{0,1},{1,2},{2,3},{3,4},{4,5},{5,6},{6,7},{7,8},{8,9},{9,10},{10,1... | collective-permute-start | bytes 1572872 | tf_op jit(solution)/shard_map/ppermute | solution.py:24
  94.7 54.6 %collective-permute-start.5 = (bf16[256,1024]{0,1:T(8,128)(2,1)}, bf16[256,1024]{0,1:T(8,128)(2,1)}, u32[]{:S(2)}, u32[]{:S(2)}) collective-permute-start(bf16[256,1024]{0,1:T(8,128)(2,1)} %collective-permute-done.2), channel_id=1, source_target_pairs={{0,1},{1,2},{2,3},{3,4},{4,5},{5,6},{6,7},{7,8},{8,9},{9,10},{10,1... | collective-permute-start | bytes 1572872 | tf_op jit(solution)/shard_map/ppermute | solution.py:24
  146.0 93.0 %copy-start.9 = (f32[8,8,256]{2,1,0:T(8,128)}, f32[8,8,256]{2,1,0:T(8,128)S(1)}, u32[]{:S(2)}) copy-start(f32[8,8,256]{2,1,0:T(8,128)S(1)} %get-tuple-element.53) | copy-start | bytes 196612
  146.1 20.7 %collective-permute-start.7 = (bf16[256,1024]{0,1:T(8,128)(2,1)}, bf16[256,1024]{0,1:T(8,128)(2,1)S(1)}, u32[]{:S(2)}, u32[]{:S(2)}) collective-permute-start(bf16[256,1024]{0,1:T(8,128)(2,1)} %collective-permute-done.4), channel_id=1, source_target_pairs={{0,1},{1,2},{2,3},{3,4},{4,5},{5,6},{6,7},{7,8},{8,9},{9,10},{10,1... | collective-permute-start | bytes 1572872 | tf_op jit(solution)/shard_map/ppermute | solution.py:24
  149.3 23.2 %collective-permute-start.8 = (bf16[256,1024]{0,1:T(8,128)(2,1)}, bf16[256,1024]{0,1:T(8,128)(2,1)S(1)}, u32[]{:S(2)}, u32[]{:S(2)}) collective-permute-start(bf16[256,1024]{0,1:T(8,128)(2,1)} %collective-permute-done.5), channel_id=1, source_target_pairs={{0,1},{1,2},{2,3},{3,4},{4,5},{5,6},{6,7},{7,8},{8,9},{9,10},{10,1... | collective-permute-start | bytes 1572872 | tf_op jit(solution)/shard_map/ppermute | solution.py:24
  166.8 72.3 %copy-start.11 = (f32[8,8,256]{2,1,0:T(8,128)}, f32[8,8,256]{2,1,0:T(8,128)S(1)}, u32[]{:S(2)}) copy-start(f32[8,8,256]{2,1,0:T(8,128)S(1)} %get-tuple-element.49) | copy-start | bytes 196612
  166.8 17.7 %collective-permute-start.10 = (bf16[256,1024]{0,1:T(8,128)(2,1)S(1)}, bf16[256,1024]{0,1:T(8,128)(2,1)S(1)}, u32[]{:S(2)}, u32[]{:S(2)}) collective-permute-start(bf16[256,1024]{0,1:T(8,128)(2,1)S(1)} %collective-permute-done.7), channel_id=1, source_target_pairs={{0,1},{1,2},{2,3},{3,4},{4,5},{5,6},{6,7},{7,8},{8,9},{9,10},{10,1... | collective-permute-start | bytes 1572872 | tf_op jit(solution)/shard_map/ppermute | solution.py:24
  172.5 23.2 %collective-permute-start.11 = (bf16[256,1024]{0,1:T(8,128)(2,1)S(1)}, bf16[256,1024]{0,1:T(8,128)(2,1)S(1)}, u32[]{:S(2)}, u32[]{:S(2)}) collective-permute-start(bf16[256,1024]{0,1:T(8,128)(2,1)S(1)} %collective-permute-done.8), channel_id=1, source_target_pairs={{0,1},{1,2},{2,3},{3,4},{4,5},{5,6},{6,7},{7,8},{8,9},{9,10},{10,1... | collective-permute-start | bytes 1572872 | tf_op jit(solution)/shard_map/ppermute | solution.py:24
  184.5 22.5 %collective-permute-start.13 = (bf16[256,1024]{0,1:T(8,128)(2,1)S(1)}, bf16[256,1024]{0,1:T(8,128)(2,1)S(1)}, u32[]{:S(2)}, u32[]{:S(2)}) collective-permute-start(bf16[256,1024]{0,1:T(8,128)(2,1)S(1)} %collective-permute-done.10), channel_id=1, source_target_pairs={{0,1},{1,2},{2,3},{3,4},{4,5},{5,6},{6,7},{7,8},{8,9},{9,10},{10,1... | collective-permute-start | bytes 1572872 | tf_op jit(solution)/shard_map/ppermute | solution.py:24
  195.7 22.6 %collective-permute-start.14 = (bf16[256,1024]{0,1:T(8,128)(2,1)S(1)}, bf16[256,1024]{0,1:T(8,128)(2,1)}, u32[]{:S(2)}, u32[]{:S(2)}) collective-permute-start(bf16[256,1024]{0,1:T(8,128)(2,1)S(1)} %collective-permute-done.11), channel_id=1, source_target_pairs={{0,1},{1,2},{2,3},{3,4},{4,5},{5,6},{6,7},{7,8},{8,9},{9,10},{10,1... | collective-permute-start | bytes 1572872 | tf_op jit(solution)/shard_map/ppermute | solution.py:24
  206.9 22.9 %collective-permute-start.16 = (bf16[256,1024]{0,1:T(8,128)(2,1)S(1)}, bf16[256,1024]{0,1:T(8,128)(2,1)S(1)}, u32[]{:S(2)}, u32[]{:S(2)}) collective-permute-start(bf16[256,1024]{0,1:T(8,128)(2,1)S(1)} %collective-permute-done.13), channel_id=1, source_target_pairs={{0,1},{1,2},{2,3},{3,4},{4,5},{5,6},{6,7},{7,8},{8,9},{9,10},{10,1... | collective-permute-start | bytes 1572872 | tf_op jit(solution)/shard_map/ppermute | solution.py:24
  218.3 163.0 %collective-permute-start.17 = (bf16[256,1024]{0,1:T(8,128)(2,1)}, bf16[256,1024]{0,1:T(8,128)(2,1)}, u32[]{:S(2)}, u32[]{:S(2)}) collective-permute-start(bf16[256,1024]{0,1:T(8,128)(2,1)} %collective-permute-done.14), channel_id=1, source_target_pairs={{0,1},{1,2},{2,3},{3,4},{4,5},{5,6},{6,7},{7,8},{8,9},{9,10},{10,1... | collective-permute-start | bytes 1572872 | tf_op jit(solution)/shard_map/ppermute | solution.py:24
  428.2 12.7 %collective-permute-start.18 = (bf16[256,8192]{1,0:T(8,128)(2,1)}, bf16[256,8192]{1,0:T(8,128)(2,1)}, u32[]{:S(2)}, u32[]{:S(2)}) collective-permute-start(bf16[256,8192]{1,0:T(8,128)(2,1)} %add_convert_fusion.1), channel_id=1, source_target_pairs={{0,16},{1,17},{2,18},{3,19},{4,20},{5,21},{6,22},{7,23},{8,24},{9,... | collective-permute-start | bytes 12582920 | tf_op jit(solution)/shard_map/ppermute | solution.py:24
  (39 other events, 698.9 us)
Sparse Core Ops, SparseCore 0:
  20.5 117.9 all-reduce.2
where the time goes:
time: 466 us; the launch traced here: 457 us
  matrix products  199 us (43%)
  other arithmetic  81.8 us (18%)
  waiting for transfers between devices  71.8 us (15%)
  starting transfers between devices  49 us (11%)
  blocking collectives  21 us (5%)
  local copies, waits for them, and re-layouts  19.7 us (4%)
  between operations  14.7 us (3%)
    dot_general x8, matrix products, fold_block(): jnp.einsum('kgts,skd->tkgd', weights.astype(jnp.bfloat16), value_heads, p...  117 us
    dot_general x8, matrix products, fold_block(): jnp.einsum('tkgd,skd->kgts', query_heads, key_heads, preferred_element_ty...  82.7 us
    reduce_sum x4, other arithmetic, fold_block(): totals = totals * factor + jnp.sum(weights, axis=-1)  54.4 us
    ppermute x19, starting transfers between devices, passed_along(): return lax.ppermute(array, axis, pairs)  49 us
    ppermute x19, waiting for transfers between devices, passed_along(): return lax.ppermute(array, axis, pairs)  44.8 us
    psum x1, waiting for transfers between devices, spread(): return lax.psum(jnp.where(mine, array, jnp.zeros_like(array)), axis)  27 us
    psum x1, blocking collectives, spread(): return lax.psum(jnp.where(mine, array, jnp.zeros_like(array)), axis)  21 us
  transfers between devices with their start and end apart: 20, of which 10 were waited for; matrix products, arithmetic and copies ran while one was open for 53% of the time, Pallas kernels for 0%

commit v1 on v0

v1 whole, which is shorter than its diff:
```python
import functools
import math

import jax
import jax.numpy as jnp
from jax import lax
from jax.experimental import pallas as pl
from jax.experimental.pallas import tpu as pltpu
from jax.sharding import PartitionSpec as P

D = 8192
QH = 64
KVH = 8
HD = 128
REACH = 6
TOK = 256
PROMPT = 128
GROUP = QH // KVH
PIECES = 2 * KVH
KEYS = PROMPT + (REACH + 1) * TOK
NEG_FILL = -1e30
SCALE = HD ** (-0.5) * math.log2(math.e)
MESH = pl.DeviceIdType.MESH

ROUTES = {
    0: {4: "zy", 3: "xx", 2: "yy", 1: "xy", 6: "zz", 5: "zz"},
    1: {1: "xx", 5: "xx", 4: "zz", 3: "yy", 2: "yy", 6: "zz"},
    2: {2: "yy", 1: "xx", 6: "yz", 5: "zz", 4: "zz", 3: "xx"},
    3: {3: "xx", 2: "yy", 1: "xx", 6: "yy", 5: "zz", 4: "zz"},
}


def upstream(c, way):
    if way == "z":
        return c, 4
    other = c ^ (1 if way == "x" else 2)
    return other, c - other


def stage_of(c, k, kv):
    if k == 0:
        return 0
    other, delta = upstream(c, ROUTES[c][k][kv])
    return stage_of(other, k - delta, kv) + 1


def sends_of(c, kv):
    found = []
    for target in range(4):
        for k, ways in ROUTES[target].items():
            other, delta = upstream(target, ways[kv])
            if other == c:
                found.append((delta, k - delta, k, stage_of(c, k - delta, kv)))
    return found


SENDS = {(c, kv): sends_of(c, kv) for c in range(4) for kv in range(2)}
MAX_SENDS = max(len(v) for v in SENDS.values())
LAST_STAGE = max(stage_of(c, k, kv) for c in range(4) for k in ROUTES[c] for kv in range(2))


def rows_of(k):
    return pl.ds(PROMPT + (REACH - k) * TOK, TOK)


def kernel(n, hidden_ref, q_ref, k_ref, v_ref, len_ref, seg_ref, out_ref,
           buf, qbuf, hbuf, obuf, cbuf, bias, segs,
           load_sem, q_sem, h_sem, o_sem, send_sem, recv_sem, psend_sem, precv_sem,
           seg_send, seg_recv, pass_send):
    me = lax.axis_index("ctx")
    section = lax.axis_index("section")
    c = lax.rem(me, 4)
    z = me // 4
    planes = n // 4
    prompt_lag = planes + 1
    lag = max(LAST_STAGE - 1, prompt_lag)

    def load(i):
        h, kv = i // 2, i % 2
        source = (k_ref, v_ref)[kv]
        return pltpu.make_async_copy(
            source.at[0, :, pl.ds(h * HD, HD)], buf.at[i, rows_of(0)], load_sem.at[i])

    def q_load(h):
        return pltpu.make_async_copy(
            q_ref.at[0, :, pl.ds(pl.multiple_of(h * GROUP * HD, GROUP * HD), GROUP * HD)],
            qbuf.at[h], q_sem.at[h])

    def hidden_load(h):
        return pltpu.make_async_copy(
            hidden_ref.at[:, pl.ds(pl.multiple_of(h * GROUP * HD, GROUP * HD), GROUP * HD)],
            hbuf.at[h], h_sem.at[h])

    def out_store(h):
        return pltpu.make_async_copy(
            obuf.at[h],
            out_ref.at[0, :, pl.ds(pl.multiple_of(h * GROUP * HD, GROUP * HD), GROUP * HD)],
            o_sem.at[h])

    def hand_over(h):
        return pltpu.make_async_remote_copy(
            src_ref=obuf.at[h], dst_ref=hbuf.at[h], send_sem=pass_send.at[h],
            recv_sem=h_sem.at[h], device_id={"section": 1 - section}, device_id_type=MESH)

    def block_copy(i, slot, delta, k_from, k_to):
        return pltpu.make_async_remote_copy(
            src_ref=buf.at[i, rows_of(k_from)], dst_ref=buf.at[i, rows_of(k_to)],
            send_sem=send_sem.at[slot, i], recv_sem=recv_sem.at[k_to - 1, i],
            device_id={"ctx": me + delta}, device_id_type=MESH)

    def prompt_copy(i, slot, delta, source):
        return pltpu.make_async_remote_copy(
            src_ref=buf.at[i, source], dst_ref=buf.at[i, pl.ds(0, PROMPT)],
            send_sem=psend_sem.at[slot, i], recv_sem=precv_sem.at[i],
            device_id={"ctx": me + delta}, device_id_type=MESH)

    def seg_copy(k):
        return pltpu.make_async_remote_copy(
            src_ref=segs.at[0], dst_ref=segs.at[k], send_sem=seg_send.at[k - 1],
            recv_sem=seg_recv.at[k - 1], device_id={"ctx": me + k}, device_id_type=MESH)

    for i in range(PIECES):
        load(i).start()
    segs[0] = seg_ref[...]

    barrier = pltpu.get_barrier_semaphore()
    pl.semaphore_signal(barrier, inc=1, device_id={"section": 1 - section}, device_id_type=MESH)
    for k in range(1, REACH + 1):
        @pl.when(me + k < n)
        def _():
            pl.semaphore_signal(barrier, inc=1, device_id={"ctx": me + k}, device_id_type=MESH)

        @pl.when(me - k >= 0)
        def _():
            pl.semaphore_signal(barrier, inc=1, device_id={"ctx": me - k}, device_id_type=MESH)
    pl.semaphore_wait(barrier, 1 + jnp.minimum(REACH, me) + jnp.minimum(REACH, n - 1 - me))

    for k in range(1, REACH + 1):
        @pl.when(me + k < n)
        def _():
            seg_copy(k).start()

    takes_prompt = (me == 5) | (me >= 7)
    prompt_stage = z + 1 + jnp.where(c == 1, 0, jnp.where(c == 2, 2, 1))
    prompt_sends = {
        1: [(4, lambda: z + 1 < planes), (-1, lambda: z >= 2), (2, lambda: z >= 1)],
        0: [(2, lambda: z >= 2)],
    }

    def each_send(cc, kv, action, stages, i):
        for slot, (delta, k_from, k_to, stage) in enumerate(SENDS[cc, kv]):
            if stage not in stages:
                continue
            good = me >= k_from
            if delta == 4:
                good = good & (z + 1 < planes)

            @pl.when(good)
            def _():
                action(block_copy(i, slot, delta, k_from, k_to))

    def at_corner(cc, body):
        @pl.when(c == cc)
        def _():
            body(cc)

    def own_sends(i):
        kv = i % 2
        load(i).wait()
        for cc in range(4):
            at_corner(cc, lambda cc: each_send(cc, kv, lambda x: x.start(), (0,), i))

    for i in range(PIECES):
        own_sends(i)

    for h in range(KVH):
        q_load(h).start()

    @pl.when(section == 0)
    def _():
        for h in range(KVH):
            hidden_load(h).start()

    for k in range(1, REACH + 1):
        @pl.when(me < k)
        def _():
            @pl.loop(0, PIECES)
            def _(i):
                buf[i, rows_of(k)] = jnp.zeros((TOK, HD), jnp.bfloat16)
            segs[k] = jnp.zeros((1, TOK), jnp.int32)

    for k in range(1, REACH + 1):
        @pl.when(me >= k)
        def _():
            seg_copy(k).wait_recv()

    own_row = segs[0]
    row = lax.broadcasted_iota(jnp.int32, (TOK, TOK), 0)
    col = lax.broadcasted_iota(jnp.int32, (TOK, TOK), 1)
    own_col = jnp.sum(
        jnp.where(row == col, jnp.broadcast_to(own_row, (TOK, TOK)), 0).astype(jnp.float32),
        axis=1, keepdims=True).astype(jnp.int32)
    bias[:, :PROMPT] = jnp.broadcast_to(
        jnp.where(own_col != 0, 0.0, NEG_FILL), (TOK, PROMPT)).astype(jnp.float32)
    for k in range(REACH + 1):
        filled = jnp.where(me >= k, len_ref[jnp.maximum(me - k, 0)], 0)
        seen = (col < filled) & (segs[k] == own_col)
        if k == 0:
            seen = seen & (col <= row)
        bias[:, PROMPT + (REACH - k) * TOK:PROMPT + (REACH - k + 1) * TOK] = jnp.where(
            seen, 0.0, NEG_FILL)
    query_len = len_ref[me]

    def communicate(p, parity):
        for stage in range(1, LAST_STAGE + 1):
            i = p - (stage - 1)
            kv = (parity - (stage - 1)) % 2

            @pl.when((i >= 0) & (i < PIECES))
            def _():
                def relay(cc):
                    for k in ROUTES[cc]:
                        if stage_of(cc, k, kv) != stage:
                            continue

                        @pl.when(me >= k)
                        def _():
                            block_copy(i, 0, 0, 0, k).wait_recv()
                    each_send(cc, kv, lambda x: x.start(), (stage,), i)
                for cc in range(4):
                    at_corner(cc, relay)

        j = p - (prompt_stage - 1)
        good = (j >= 0) & (j < PIECES)

        @pl.when(good & takes_prompt)
        def _():
            prompt_copy(j, 0, 0, pl.ds(0, PROMPT)).wait_recv()

        for cc, targets in prompt_sends.items():
            for slot, (delta, rule) in enumerate(targets):
                @pl.when(good & (c == cc) & (z >= 1) & rule())
                def _():
                    prompt_copy(j, slot, delta, pl.ds(0, PROMPT)).start()

        @pl.when(good & (me == 1))
        def _():
            prompt_copy(j, 0, 4, pl.ds(PROMPT + (REACH - 1) * TOK, PROMPT)).start()

    valid = lax.broadcasted_iota(jnp.int32, (TOK, HD), 0) < query_len

    def heads(h, first, count):
        @pl.loop(first, first + count)
        def _(g):
            lanes = pl.ds(pl.multiple_of(g * HD, HD), HD)
            scores = lax.dot_general(
                qbuf[h, :, lanes], buf[2 * h], (((1,), (1,)), ((), ())),
                preferred_element_type=jnp.float32)
            scores = scores * SCALE + bias[...]
            top = jnp.max(scores, axis=1, keepdims=True)
            weights = jnp.exp2(scores - top).astype(jnp.bfloat16)
            values = jnp.concatenate(
                [buf[2 * h + 1], jnp.ones((KEYS, HD), jnp.bfloat16)], axis=1)
            mixed = jnp.dot(weights, values, preferred_element_type=jnp.float32)
            cbuf[h, :, lanes] = jnp.where(valid, mixed[:, :HD] / mixed[:, HD:], 0.0)

    def finish(h):
        @pl.loop(0, GROUP)
        def _(g):
            lanes = pl.ds(pl.multiple_of(g * HD, HD), HD)
            obuf[h, :, lanes] = (
                hbuf[h, :, lanes].astype(jnp.float32) + cbuf[h, :, lanes]).astype(jnp.bfloat16)
        out_store(h).start()

    def finish_first(h):
        hidden_load(h).wait()
        finish(h)
        hand_over(h).start()

    def finish_second(h):
        hand_over(h).wait_recv()
        finish(h)

    @pl.loop(0, (lag + 1) // 2 + KVH + 1)
    def _(t):
        start_phase = (lag + 1) // 2
        for parity in range(2):
            communicate(2 * t + parity, parity)
            half = (parity + lag + 1) % 2
            h = t - start_phase - (1 if lag % 2 == 0 and half == 1 else 0)

            @pl.when((h >= 0) & (h < KVH))
            def _():
                if half == 0:
                    q_load(h).wait()

                    @pl.when((me < 5) | (me == 6))
                    def _():
                        block0 = pl.ds(
                            pl.multiple_of(PROMPT + (REACH - me) * TOK, PROMPT), PROMPT)
                        buf[2 * h, :PROMPT] = buf[2 * h, block0]
                        buf[2 * h + 1, :PROMPT] = buf[2 * h + 1, block0]
                heads(h, half * (GROUP // 2), GROUP // 2)
                if half == 1:
                    @pl.when(section == 0)
                    def _():
                        finish_first(h)

                    @pl.when((section == 1) & (h >= 1))
                    def _():
                        finish_second(h - 1)

    @pl.when(section == 1)
    def _():
        finish_second(KVH - 1)

    for k in range(1, REACH + 1):
        @pl.when(me + k < n)
        def _():
            seg_copy(k).wait_send()

    @pl.loop(0, KVH)
    def _(h):
        out_store(h).wait()

        @pl.when(section == 0)
        def _():
            hand_over(h).wait_send()
        for kv in range(2):
            i = 2 * h + kv
            for cc in range(4):
                at_corner(cc, lambda cc: each_send(
                    cc, kv, lambda x: x.wait_send(), range(LAST_STAGE + 1), i))
            for cc, targets in prompt_sends.items():
                for slot, (delta, rule) in enumerate(targets):
                    @pl.when((c == cc) & (z >= 1) & rule())
                    def _():
                        prompt_copy(i, slot, delta, pl.ds(0, PROMPT)).wait_send()

            @pl.when(me == 1)
            def _():
                prompt_copy(i, 0, 4, pl.ds(0, PROMPT)).wait_send()


def local(n, hidden_in, query_rows, key_rows, value_rows, stretch_len, segment_ids):
    anywhere = pl.BlockSpec(memory_space=pl.ANY)
    wide = GROUP * HD
    dma = pltpu.SemaphoreType.DMA
    return pl.pallas_call(
        functools.partial(kernel, n),
        out_shape=jax.ShapeDtypeStruct((1, TOK, D), jnp.bfloat16),
        in_specs=[anywhere] * 4 + [
            pl.BlockSpec(memory_space=pltpu.SMEM), pl.BlockSpec(memory_space=pltpu.VMEM)],
        out_specs=anywhere,
        scratch_shapes=[
            pltpu.VMEM((PIECES, KEYS, HD), jnp.bfloat16),
            pltpu.VMEM((KVH, TOK, wide), jnp.bfloat16),
            pltpu.VMEM((KVH, TOK, wide), jnp.bfloat16),
            pltpu.VMEM((KVH, TOK, wide), jnp.bfloat16),
            pltpu.VMEM((KVH, TOK, wide), jnp.float32),
            pltpu.VMEM((TOK, KEYS), jnp.float32),
            pltpu.VMEM((REACH + 1, 1, TOK), jnp.int32),
            dma((PIECES,)),
            dma((KVH,)),
            dma((KVH,)),
            dma((KVH,)),
            dma((MAX_SENDS, PIECES)),
            dma((REACH, PIECES)),
            dma((3, PIECES)),
            dma((PIECES,)),
            dma((REACH,)),
            dma((REACH,)),
            dma((KVH,)),
        ],
        compiler_params=pltpu.CompilerParams(
            collective_id=0, has_side_effects=True, vmem_limit_bytes=56 * 1024 * 1024),
    )(hidden_in, query_rows, key_rows, value_rows, stretch_len, segment_ids.reshape(1, TOK))


def solution(mesh):
    return jax.shard_map(
        functools.partial(local, mesh.shape["ctx"]),
        mesh=mesh,
        in_specs=(
            P("ctx", None),
            P("section", "ctx", None),
            P("section", "ctx", None),
            P("section", "ctx", None),
            P(),
            P("ctx"),
        ),
        out_specs=P("section", "ctx", None),
        check_vma=False,
    )
```

time: 466 us -> 151 us (0.32); the launches traced: 457 us -> 151 us
  matrix products: 199 us -> 0 us
  Pallas kernels: 0 us -> 146 us
  other arithmetic: 81.8 us -> 0 us
  waiting for transfers between devices: 71.8 us -> 0 us
  starting transfers between devices: 49 us -> 0 us
  blocking collectives: 21 us -> 0 us
  local copies, waits for them, and re-layouts: 19.7 us -> 4.64 us
  between operations: 14.7 us -> 0.01 us
    dot_general x16 -> x0, matrix products: 199 us -> none  [the longest x8 117 us: fold_block(): jnp.einsum('kgts,skd->tkgd', weights.astype(jnp.bfloat16), value_heads, p...]
    pallas_call x0 -> x1, Pallas kernels: none -> 146 us  [local(): pl.pallas_call(functools.partial(kernel, n), out_shape=jax.ShapeDtypeStru...]
    reduce_sum x4 -> x0, other arithmetic: 54.4 us -> none  [fold_block(): totals = totals * factor + jnp.sum(weights, axis=-1)]
    ppermute x19 -> x0, starting transfers between devices: 49 us -> none  [passed_along(): return lax.ppermute(array, axis, pairs)]
    ppermute x19 -> x0, waiting for transfers between devices: 44.8 us -> none  [passed_along(): return lax.ppermute(array, axis, pairs)]
    psum x1 -> x0, waiting for transfers between devices: 27 us -> none  [spread(): return lax.psum(jnp.where(mine, array, jnp.zeros_like(array)), axis)]
    psum x1 -> x0, blocking collectives: 21 us -> none  [spread(): return lax.psum(jnp.where(mine, array, jnp.zeros_like(array)), axis)]
    reshape x2 -> x0, local copies, waits for them, and re-layouts: 9.97 us -> none  [the longest x1 8.94 us: local(): (mixed_sum / jnp.transpose(totals, (2, 0, 1))[..., None]).reshape(tok_cou...]
  transfers between devices with their start and end apart: 20 -> 0, of which waited for: 10 -> 0; matrix products, arithmetic and copies ran while one was open for 53% -> 0% of each run, Pallas kernels for 0% -> 0%
where the time goes in v1:
time: 151 us
  Pallas kernels  146 us (97%)
  local copies, waits for them, and re-layouts  4.64 us (3%)
    pallas_call x1, Pallas kernels, local(): pl.pallas_call(functools.partial(kernel, n), out_shape=jax.ShapeDtypeStru...  146 us
    unnamed x1, local copies, waits for them, and re-layouts  4.64 us

profile of v1, /device:TPU:17, one launch (start us, length us, event | category | flops | bytes accessed | tf_op | source)
XLA Modules:
  0.0 150.7 jit_solution(1945240078171460282)
XLA Ops:
  0.0 146.1 %shard_map.64 = bf16[1,256,8192]{2,1,0:T(8,128)(2,1)} custom-call(bf16[256,8192]{1,0:T(8,128)(2,1)} %hidden_ref.1, bf16[1,256,8192]{2,1,0:T(8,128)(2,1)} %q_ref.1, bf16[1,256,1024]{2,1,0:T(8,128)(2,1)} %k_ref.1, bf16[1,256,1024]{2,1,0:T(8,128)(2,1)} %v_ref.1, s32[16]{0:T(128)} %len_ref.1, s32[1,256]{1,0:T(1,128)} %bitcast.1), custom_call_target="tpu_custom_call" | custom-call | tf_op jit(solution)/shard_map/pallas_call | solution.py:349
  146.1 4.6 %copy.8 = bf16[1,256,8192]{2,1,0:T(8,128)(2,1)} copy(bf16[1,256,8192]{2,1,0:T(8,128)(2,1)} %shard_map.64) | data formatting | bytes 8388608

commit v2 on v1

--- a/solution.py
+++ b/solution.py
@@ -19,6 +19,7 @@
 PIECES = 2 * KVH
 KEYS = PROMPT + (REACH + 1) * TOK
 NEG_FILL = -1e30
+LEAD = 2
 SCALE = HD ** (-0.5) * math.log2(math.e)
 MESH = pl.DeviceIdType.MESH
 
@@ -75,11 +76,10 @@
     prompt_lag = planes + 1
     lag = max(LAST_STAGE - 1, prompt_lag)
 
-    def load(i):
-        h, kv = i // 2, i % 2
+    def load(i, kv):
         source = (k_ref, v_ref)[kv]
         return pltpu.make_async_copy(
-            source.at[0, :, pl.ds(h * HD, HD)], buf.at[i, rows_of(0)], load_sem.at[i])
+            source.at[0, :, pl.ds(pl.multiple_of((i // 2) * HD, HD), HD)], buf.at[i, rows_of(0)], load_sem.at[i])
 
     def q_load(h):
         return pltpu.make_async_copy(
@@ -120,7 +120,7 @@
             recv_sem=seg_recv.at[k - 1], device_id={"ctx": me + k}, device_id_type=MESH)
 
     for i in range(PIECES):
-        load(i).start()
+        load(i, i % 2).start()
     segs[0] = seg_ref[...]
 
     barrier = pltpu.get_barrier_semaphore()
@@ -164,14 +164,13 @@
         def _():
             body(cc)
 
-    def own_sends(i):
-        kv = i % 2
-        load(i).wait()
+    def own_sends(i, kv):
+        load(i, kv).wait()
         for cc in range(4):
             at_corner(cc, lambda cc: each_send(cc, kv, lambda x: x.start(), (0,), i))
 
-    for i in range(PIECES):
-        own_sends(i)
+    for i in range(LEAD):
+        own_sends(i, i % 2)
 
     for h in range(KVH):
         q_load(h).start()
@@ -212,6 +211,10 @@
     query_len = len_ref[me]
 
     def communicate(p, parity):
+        @pl.when(p + LEAD < PIECES)
+        def _():
+            own_sends(p + LEAD, (parity + LEAD) % 2)
+
         for stage in range(1, LAST_STAGE + 1):
             i = p - (stage - 1)
             kv = (parity - (stage - 1)) % 2
@@ -250,19 +253,20 @@
     valid = lax.broadcasted_iota(jnp.int32, (TOK, HD), 0) < query_len
 
     def heads(h, first, count):
-        @pl.loop(first, first + count)
-        def _(g):
-            lanes = pl.ds(pl.multiple_of(g * HD, HD), HD)
+        def scores_of(g):
             scores = lax.dot_general(
-                qbuf[h, :, lanes], buf[2 * h], (((1,), (1,)), ((), ())),
+                qbuf[h, :, g * HD:(g + 1) * HD], buf[2 * h], (((1,), (1,)), ((), ())),
                 preferred_element_type=jnp.float32)
-            scores = scores * SCALE + bias[...]
+            return scores * SCALE + bias[...]
+
+        all_scores = [scores_of(g) for g in range(first, first + count)]
+        for g, scores in zip(range(first, first + count), all_scores):
             top = jnp.max(scores, axis=1, keepdims=True)
             weights = jnp.exp2(scores - top).astype(jnp.bfloat16)
             values = jnp.concatenate(
                 [buf[2 * h + 1], jnp.ones((KEYS, HD), jnp.bfloat16)], axis=1)
             mixed = jnp.dot(weights, values, preferred_element_type=jnp.float32)
-            cbuf[h, :, lanes] = jnp.where(valid, mixed[:, :HD] / mixed[:, HD:], 0.0)
+            cbuf[h, :, g * HD:(g + 1) * HD] = jnp.where(valid, mixed[:, :HD] / mixed[:, HD:], 0.0)
 
     def finish(h):
         @pl.loop(0, GROUP)

time: 151 us -> 99.8 us (0.66)
  Pallas kernels: 146 us -> 94.9 us
    pallas_call x1, Pallas kernels: 146 us -> 94.9 us  [local(): pl.pallas_call(functools.partial(kernel, n), out_shape=jax.ShapeDtypeStru...]
where the time goes in v2:
time: 99.8 us; the launch traced here: 99.5 us
  Pallas kernels  94.9 us (95%)
  local copies, waits for them, and re-layouts  4.64 us (5%)
    pallas_call x1, Pallas kernels, local(): pl.pallas_call(functools.partial(kernel, n), out_shape=jax.ShapeDtypeStru...  94.9 us
    unnamed x1, local copies, waits for them, and re-layouts  4.64 us

profile of v2, /device:TPU:17, one launch (start us, length us, event | category | flops | bytes accessed | tf_op | source)
XLA Modules:
  0.0 99.5 jit_solution(15570457228478110745)
XLA Ops:
  0.0 94.9 %shard_map.64 = bf16[1,256,8192]{2,1,0:T(8,128)(2,1)} custom-call(bf16[256,8192]{1,0:T(8,128)(2,1)} %hidden_ref.1, bf16[1,256,8192]{2,1,0:T(8,128)(2,1)} %q_ref.1, bf16[1,256,1024]{2,1,0:T(8,128)(2,1)} %k_ref.1, bf16[1,256,1024]{2,1,0:T(8,128)(2,1)} %v_ref.1, s32[16]{0:T(128)} %len_ref.1, s32[1,256]{1,0:T(1,128)} %bitcast.1), custom_call_target="tpu_custom_call" | custom-call | tf_op jit(solution)/shard_map/pallas_call | solution.py:353
  94.9 4.6 %copy.8 = bf16[1,256,8192]{2,1,0:T(8,128)(2,1)} copy(bf16[1,256,8192]{2,1,0:T(8,128)(2,1)} %shard_map.64) | data formatting | bytes 8388608
